TPU v7x, 32 devices: a whole 2x2x4 slice. The times are simulated.
32 devices in a mesh: dp: 4 (over z), tensor: 8 (over y, x, core).
Axes of the slice: x: 2, y: 2, z: 4, core: 2. Of those that a mesh axis runs over, the one named last changes fastest.
Arguments:
- activations: bfloat16 [64, 8192], P('dp'), may hold values from -6 to 6
- query_weight: bfloat16 [8192, 8192], P(None, 'tensor'), may hold values from -0.0625 to 0.0625
- output_weight: bfloat16 [8192, 8192], P('tensor'), may hold values from -0.375 to 0.375
- key_cache: bfloat16 [64, 8, 1024, 128], P(('dp', 'tensor'))
- value_cache: bfloat16 [64, 8, 1024, 128], P(('dp', 'tensor')), may hold values from -6 to 6
- fresh_pair: bfloat16 [64, 2, 1024], P(('dp', 'tensor')), may hold values from -6 to 6
- cache_length: int32 [64], P(('dp', 'tensor')), may hold values from 2 to 1024
- row_tenant: int32 [64], P('dp'), may hold values from 0 to 31, as said below
- tenant_slot: int32 [32], replicated, may hold values from 0 to 31, as said below
- query_deltas: bfloat16 [32, 64, 128, 128], P('dp', 'tensor'), may hold values from -0.1796875 to 0.1796875
- query_where: int32 [32, 64], P('dp', 'tensor'), may hold values from 0 to 511, as said below
- output_deltas: bfloat16 [32, 64, 128, 128], P('dp', 'tensor'), may hold values from -0.71875 to 0.71875
- output_where: int32 [32, 64], P('dp', 'tensor'), may hold values from 0 to 511, as said below
Outputs:
- layer_out: bfloat16 [64, 8192], P('dp', 'tensor')
Inputs may be any that keep to these rules, and one draw needn't show every extreme that they name: A permutation: tenant t's tiles sit in slot tenant_slot[t], on dp index tenant_slot[t] // 8. `row_tenant`: among the requests of one dp group (16 consecutive rows), at most 8 have tenants stored on one dp index; one store receives exactly 8 from every group. `query_where`: within each block of 8 entries (one slot, one shard) the places are distinct. `output_where`: within each block of 8 entries (one slot, one shard) the places are distinct.
All inputs are finite; a program needn't handle non-finite values.
Results may differ from a plain program's by a relative error of at most 0.0089.
Values may be sent and summed in bfloat16 or wider, within the bound.
A program may use at most 192 MiB of HBM per device.

v0:
```python
import jax
import jax.numpy as jnp
from jax import lax
from jax.sharding import PartitionSpec as P


def apply_tiles(inputs, row_slot, deltas, where_list, first_slot, out_columns):
    tile_size = deltas.shape[-1]
    slot_count = where_list.shape[0]
    per_slot = where_list.shape[1]
    out_tiles = out_columns // tile_size
    count_rows = inputs.shape[0]
    in_tiles = inputs.shape[1] // tile_size
    blocks = inputs.reshape(count_rows, in_tiles, tile_size)
    flat_places = where_list.reshape(slot_count * per_slot)
    source = flat_places // out_tiles
    target = flat_places % out_tiles
    pick_table = (source[:, None] == jnp.arange(in_tiles, dtype=jnp.int32)[None, :]).astype(
        inputs.dtype
    )
    picked = jnp.einsum(
        "rbt,kb->rkt", blocks, pick_table, preferred_element_type=jnp.float32
    ).astype(inputs.dtype)
    owners = first_slot + jnp.arange(slot_count * per_slot, dtype=jnp.int32) // per_slot
    chosen = row_slot[:, None] == owners[None, :]
    picked = jnp.where(chosen[:, :, None], picked, jnp.zeros((), inputs.dtype))
    flat_tiles = deltas.reshape(slot_count * per_slot, tile_size, tile_size)
    products = jnp.einsum("rkt,kts->rks", picked, flat_tiles, preferred_element_type=jnp.float32)
    spread = (target[:, None] == jnp.arange(out_tiles, dtype=jnp.int32)[None, :]).astype(
        jnp.float32
    )
    combined = jnp.einsum("rks,kb->rbs", products, spread, precision=lax.Precision.HIGHEST)
    return combined.reshape(count_rows, out_columns)


def dispatch_table(row_slot, per_store, stores, capacity):
    store_of = row_slot // per_store
    row_order = jnp.arange(row_slot.shape[0], dtype=jnp.int32)
    earlier = (store_of[:, None] == store_of[None, :]) & (row_order[None, :] < row_order[:, None])
    place_in = jnp.sum(earlier.astype(jnp.int32), axis=1)
    place_at = store_of * capacity + place_in
    one_hot = place_at[None, :] == jnp.arange(stores * capacity, dtype=jnp.int32)[:, None]
    return (place_at, one_hot)


def visit_store(inputs, row_slot, one_hot, deltas, where_list, out_columns, capacity):
    stores = lax.axis_size("dp")
    packed = jnp.dot(
        one_hot.astype(inputs.dtype), inputs, preferred_element_type=jnp.float32
    ).astype(inputs.dtype)
    slot_sent = jnp.max(jnp.where(one_hot, row_slot[None, :], -1), axis=1)
    packed = packed.reshape(stores, capacity, inputs.shape[1])
    slot_sent = slot_sent.reshape(stores, capacity)
    arrived, arrived_slot = (
        lax.all_to_all(packed, "dp", split_axis=0, concat_axis=0, tiled=True),
        lax.all_to_all(slot_sent, "dp", split_axis=0, concat_axis=0, tiled=True),
    )
    first_slot = lax.axis_index("dp") * deltas.shape[0]
    result = apply_tiles(
        arrived.reshape(stores * capacity, inputs.shape[1]),
        arrived_slot.reshape(stores * capacity),
        deltas,
        where_list,
        first_slot,
        out_columns,
    )
    return result.reshape(stores, capacity, out_columns)


def return_home(result, one_hot):
    returned = lax.all_to_all(result, "dp", split_axis=0, concat_axis=0, tiled=True)
    flattened = returned.reshape(returned.shape[0] * returned.shape[1], returned.shape[2])
    return jnp.dot(one_hot.astype(jnp.float32).T, flattened, precision=lax.Precision.HIGHEST)


def attend(query_rows, key_cache, value_cache, fresh_pair, cache_length):
    count_rows, kv_heads, context, head_dim = key_cache.shape
    grouped = query_rows.reshape(count_rows, kv_heads, -1, head_dim)
    score_scale = head_dim ** (-0.5)
    scores = (
        jnp.einsum("rkgd,rkld->rkgl", grouped, key_cache, preferred_element_type=jnp.float32)
        * score_scale
    )
    fresh_key = fresh_pair[:, 0].reshape(count_rows, kv_heads, head_dim)
    fresh_value = fresh_pair[:, 1].reshape(count_rows, kv_heads, head_dim).astype(jnp.float32)
    own_score = (
        jnp.einsum("rkgd,rkd->rkg", grouped, fresh_key, preferred_element_type=jnp.float32)
        * score_scale
    )
    position = jnp.arange(context, dtype=jnp.int32)
    visible = (position[None, :] < cache_length[:, None])[:, None, None, :]
    scores = jnp.where(visible, scores, -1e30)
    highest = jnp.maximum(jnp.max(scores, axis=3), own_score)
    weights = jnp.where(visible, jnp.exp(scores - highest[..., None]), 0.0)
    own_weight = jnp.exp(own_score - highest)
    denominator = jnp.sum(weights, axis=3) + own_weight
    probabilities = (weights / denominator[..., None]).astype(jnp.bfloat16)
    own_probability = (own_weight / denominator).astype(jnp.bfloat16)
    mixed = jnp.einsum(
        "rkgl,rkld->rkgd", probabilities, value_cache, preferred_element_type=jnp.float32
    )
    mixed = mixed + own_probability.astype(jnp.float32)[..., None] * fresh_value[:, :, None, :]
    return mixed.astype(jnp.bfloat16).reshape(count_rows, -1)


def body(
    activations,
    query_weight,
    output_weight,
    key_cache,
    value_cache,
    fresh_pair,
    cache_length,
    row_tenant,
    tenant_slot,
    query_deltas,
    query_where,
    output_deltas,
    output_where,
):
    group_rows = activations.shape[0]
    stores = lax.axis_size("dp")
    capacity = max(2, 2 * group_rows // stores)
    per_store = query_deltas.shape[0]
    row_slot = jnp.take(tenant_slot, row_tenant)
    place_at, one_hot = dispatch_table(row_slot, per_store, stores, capacity)
    query_width = query_weight.shape[1]
    out_columns = output_weight.shape[1]
    base_query = jnp.dot(activations, query_weight, preferred_element_type=jnp.float32)
    query_extra = return_home(
        visit_store(
            activations, row_slot, one_hot, query_deltas, query_where, query_width, capacity
        ),
        one_hot,
    )
    query_heads = (base_query + query_extra).astype(jnp.bfloat16)
    query_rows = lax.all_to_all(query_heads, "tensor", split_axis=0, concat_axis=1, tiled=True)
    attended = attend(query_rows, key_cache, value_cache, fresh_pair, cache_length)
    heads_out = lax.all_to_all(attended, "tensor", split_axis=1, concat_axis=0, tiled=True)
    base_out = jnp.dot(heads_out, output_weight, preferred_element_type=jnp.float32)
    visited = visit_store(
        heads_out, row_slot, one_hot, output_deltas, output_where, out_columns, capacity
    )
    partial_terms = base_out + return_home(visited, one_hot)
    summed = lax.psum_scatter(partial_terms, "tensor", scatter_dimension=1, tiled=True)
    return summed.astype(jnp.bfloat16)


def solution(mesh):
    placed = (
        P("dp", None),
        P(None, "tensor"),
        P("tensor", None),
        P(("dp", "tensor"), None, None, None),
        P(("dp", "tensor"), None, None, None),
        P(("dp", "tensor"), None, None),
        P(("dp", "tensor")),
        P("dp"),
        P(),
        P("dp", "tensor", None, None),
        P("dp", "tensor"),
        P("dp", "tensor", None, None),
        P("dp", "tensor"),
    )
    return jax.shard_map(
        body, mesh=mesh, in_specs=placed, out_specs=P("dp", "tensor"), check_vma=False
    )
```

profile of v0, /device:TPU:0, one launch (start us, length us, event | category | flops | bytes accessed | tf_op | source)
XLA Modules:
  0.0 159.8 jit_solution(9952750068246785595)
XLA Ops:
  6.5 0.8 compare_select_fusion
  7.4 1.3 gather_fusion
  8.7 0.7 and_select_fusion.5
  9.3 0.2 convert_reduce_fusion
  9.5 0.1 select_reduce_fusion
  9.6 0.7 all_to_all.45
  10.3 6.3 %all-to-all-start = ((s32[4,1,8]{2,1,0:T(1,128)}), s32[4,1,8]{2,1,0:T(1,128)S(1)}, u32[]{:S(2)}, u32[]{:S(2)}) async-start(s32[4,1,8]{2,1,0:T(1,128)} %bitcast.1), calls=%async_computation | async-start | bytes 4096 | tf_op jit(solution)/shard_map/all_to_all | solution.py:56
  16.6 2.1 %fusion = bf16[4,8,8192]{2,1,0:T(8,128)(2,1)} fusion(bf16[16,8192]{1,0:T(8,128)(2,1)} %param.13, s32[16]{0:T(128)S(1)} %multiply_add_fusion), kind=kOutput, calls=%fused_computation.2 | convolution fusion | flops 8651264 | bytes 786496 | tf_op jit(solution)/shard_map/dot_general | solution.py:48
  18.8 3.3 %all-to-all-done = s32[4,1,8]{2,1,0:T(1,128)S(1)} async-done(((s32[4,1,8]{2,1,0:T(1,128)}), s32[4,1,8]{2,1,0:T(1,128)S(1)}, u32[]{:S(2)}, u32[]{:S(2)}) %all-to-all-start) | async-done | bytes 160 | tf_op jit(solution)/shard_map/all_to_all | solution.py:56
  22.1 3.5 %all-to-all-start.1 = ((bf16[4,8,8192]{2,1,0:T(8,128)(2,1)}), bf16[4,8,8192]{2,1,0:T(8,128)(2,1)S(1)}, u32[]{:S(2)}, u32[]{:S(2)}) async-start(bf16[4,8,8192]{2,1,0:T(8,128)(2,1)} %fusion), calls=%async_computation.1 | async-start | bytes 1048576 | tf_op jit(solution)/shard_map/all_to_all | solution.py:55
  25.6 8.1 %fusion.47 = f32[16,1024]{1,0:T(8,128)S(1)} fusion(bf16[16,8192]{1,0:T(8,128)(2,1)} %param.13, bf16[8192,1024]{1,0:T(8,128)(2,1)} %param.14), kind=kOutput, calls=%fused_computation.94 | convolution fusion | flops 268435456 | bytes 17104896 | tf_op jit(solution)/shard_map/dot_general | solution.py:129
  33.7 0.1 reshape.265
  33.8 0.5 broadcast.270
  34.3 0.7 reduce.3
  35.0 0.1 eq.116
  35.2 3.7 %all-to-all-done.1 = bf16[4,8,8192]{2,1,0:T(8,128)(2,1)S(1)} async-done(((bf16[4,8,8192]{2,1,0:T(8,128)(2,1)}), bf16[4,8,8192]{2,1,0:T(8,128)(2,1)S(1)}, u32[]{:S(2)}, u32[]{:S(2)}) %all-to-all-start.1) | async-done | bytes 524320 | tf_op jit(solution)/shard_map/all_to_all | solution.py:55
  38.9 0.1 copy.34
  39.0 0.4 fusion.2
  39.4 0.7 convolution_bitcast_fusion.1
  40.0 1.0 convolution_bitcast_fusion.3
  41.1 0.7 reshape_reshape.13
  41.8 3.3 %all-to-all-start.2 = ((f32[4,8,1024]{2,1,0:T(8,128)}), f32[4,8,1024]{2,1,0:T(8,128)S(1)}, u32[]{:S(2)}, u32[]{:S(2)}) async-start(f32[4,8,1024]{2,1,0:T(8,128)} %reshape_reshape.13), calls=%async_computation.2 | async-start | bytes 262144 | tf_op jit(solution)/shard_map/all_to_all | solution.py:71
  45.1 5.9 %all-to-all-done.2 = f32[4,8,1024]{2,1,0:T(8,128)S(1)} async-done(((f32[4,8,1024]{2,1,0:T(8,128)}), f32[4,8,1024]{2,1,0:T(8,128)S(1)}, u32[]{:S(2)}, u32[]{:S(2)}) %all-to-all-start.2) | async-done | bytes 131104 | tf_op jit(solution)/shard_map/all_to_all | solution.py:71
  51.0 0.2 fusion.7
  51.2 0.6 all_to_all.49
  51.8 3.7 %all-to-all-start.3 = ((bf16[8,2,1024]{2,1,0:T(2,128)(2,1)}), bf16[8,2,1024]{2,1,0:T(2,128)(2,1)S(1)}, u32[]{:S(2)}, u32[]{:S(2)}) async-start(bf16[8,2,1024]{2,1,0:T(2,128)(2,1)} %all_to_all.49), calls=%async_computation.3 | async-start | bytes 65536 | tf_op jit(solution)/shard_map/all_to_all | solution.py:137
  55.6 4.8 %all-to-all-done.3 = bf16[8,2,1024]{2,1,0:T(2,128)(2,1)S(1)} async-done(((bf16[8,2,1024]{2,1,0:T(2,128)(2,1)}), bf16[8,2,1024]{2,1,0:T(2,128)(2,1)S(1)}, u32[]{:S(2)}, u32[]{:S(2)}) %all-to-all-start.3) | async-done | bytes 32800 | tf_op jit(solution)/shard_map/all_to_all | solution.py:137
  60.5 0.1 fusion.24
  60.6 3.6 %fusion.46 = (f32[2,8,8]{2,1,0:T(8,128)S(1)}, f32[2,8,8,1024]{3,2,1,0:T(8,128)S(1)}) fusion(bf16[2,8,1024,128]{3,2,1,0:T(8,128)(2,1)} %param.16, bf16[2,8,8,128]{3,2,0,1:T(8,128)(2,1)S(1)} %reshape.290, pred[2,1024]{1,0:T(4,128)(4,1)S(1)} %iota_compare_fusion.8), kind=kOutput, calls=%fused_computation.93 | convolution fusion | flops 33947520 | bytes 4753920 | tf_op jit(solution)/shard_map/rkgd,rkld->rkgl/dot_general | solution.py:81
  64.2 0.2 fusion.14
  64.5 0.7 fusion.8
  65.2 0.6 copy.28
  65.9 3.3 %all-to-all-start.4 = ((bf16[2,8,1024]{2,0,1:T(2,128)(2,1)}), bf16[2,8,1024]{2,0,1:T(2,128)(2,1)S(1)}, u32[]{:S(2)}, u32[]{:S(2)}) async-start(bf16[2,8,1024]{2,0,1:T(2,128)(2,1)} %copy.28), calls=%async_computation.4 | async-start | bytes 65536 | tf_op jit(solution)/shard_map/all_to_all | solution.py:139
  69.3 4.7 %all-to-all-done.4 = bf16[2,8,1024]{2,0,1:T(2,128)(2,1)S(1)} async-done(((bf16[2,8,1024]{2,0,1:T(2,128)(2,1)}), bf16[2,8,1024]{2,0,1:T(2,128)(2,1)S(1)}, u32[]{:S(2)}, u32[]{:S(2)}) %all-to-all-start.4) | async-done | bytes 32800 | tf_op jit(solution)/shard_map/all_to_all | solution.py:139
  74.0 0.9 fusion.6
  74.9 3.3 %all-to-all-start.5 = ((bf16[4,8,1024]{2,1,0:T(8,128)(2,1)}), bf16[4,8,1024]{2,1,0:T(8,128)(2,1)S(1)}, u32[]{:S(2)}, u32[]{:S(2)}) async-start(bf16[4,8,1024]{2,1,0:T(8,128)(2,1)} %fusion.6), calls=%async_computation.5 | async-start | bytes 131072 | tf_op jit(solution)/shard_map/all_to_all | solution.py:55
  78.2 5.7 %all-to-all-done.5 = bf16[4,8,1024]{2,1,0:T(8,128)(2,1)S(1)} async-done(((bf16[4,8,1024]{2,1,0:T(8,128)(2,1)}), bf16[4,8,1024]{2,1,0:T(8,128)(2,1)S(1)}, u32[]{:S(2)}, u32[]{:S(2)}) %all-to-all-start.5) | async-done | bytes 65568 | tf_op jit(solution)/shard_map/all_to_all | solution.py:55
  84.0 0.4 fusion.4
  84.3 2.3 %convolution_bitcast_fusion = f32[32,64,128]{2,0,1:T(8,128)S(1)} fusion(bf16[64,128,128]{2,1,0:T(8,128)(2,1)} %bitcast.72, bf16[32,64,128]{2,1,0:T(8,128)(2,1)S(1)} %fusion.4), kind=kOutput, calls=%fused_computation.4 | convolution fusion | flops 67108864 | bytes 3670016 | tf_op jit(solution)/shard_map/rkt,kts->rks/dot_general | solution.py:28
  86.6 1.3 convolution_bitcast_fusion.2
  87.9 1.2 reshape_reshape.15
  89.1 3.5 %all-to-all-start.6 = ((f32[4,8,8192]{2,1,0:T(8,128)}), f32[4,8,8192]{2,1,0:T(8,128)S(1)}, u32[]{:S(2)}, u32[]{:S(2)}) async-start(f32[4,8,8192]{2,1,0:T(8,128)} %reshape_reshape.15), calls=%async_computation.6 | async-start | bytes 2097152 | tf_op jit(solution)/shard_map/all_to_all | solution.py:71
  92.6 0.2 reduce-scatter.2.cloned.1.call-start
  92.8 8.9 %fusion.48 = f32[16,8192]{1,0:T(8,128)} fusion(bf16[16,1024]{1,0:T(8,128)(2,1)S(1)} %all_to_all.55, bf16[1024,8192]{1,0:T(8,128)(2,1)} %param.15), kind=kOutput, calls=%fused_computation.95 | convolution fusion | flops 268435456 | bytes 17334272 | tf_op jit(solution)/shard_map/dot_general | solution.py:140
  101.7 15.6 %all-to-all-done.6 = f32[4,8,8192]{2,1,0:T(8,128)S(1)} async-done(((f32[4,8,8192]{2,1,0:T(8,128)}), f32[4,8,8192]{2,1,0:T(8,128)S(1)}, u32[]{:S(2)}, u32[]{:S(2)}) %all-to-all-start.6) | async-done | bytes 1048608 | tf_op jit(solution)/shard_map/all_to_all | solution.py:71
  117.3 2.4 %convolution_add_fusion = f32[16,8192]{1,0:T(8,128)} fusion(f32[16,8192]{1,0:T(8,128)} %fusion.48, f32[4,8,8192]{2,1,0:T(8,128)S(1)} %all-to-all-done.6, s32[16]{0:T(128)S(1)} %multiply_add_fusion), kind=kOutput, calls=%fused_computation.3 | convolution fusion | flops 50463232 | bytes 2097216 | tf_op jit(solution)/shard_map/dot_general | solution.py:73
  119.7 31.8 %reduce-scatter.2.cloned.1.call-done = f32[16,1024]{1,0:T(8,128)} async-done(((f32[16,8192]{1,0:T(8,128)}), f32[16,1024]{1,0:T(8,128)}) %reduce-scatter.2.cloned.1.call-update) | async-done | bytes 65552 | tf_op jit(solution)/shard_map/reduce_scatter | solution.py:145
  151.5 1.5 convert_element_type.71
  (28 shorter events, 0.4 us)
Async XLA Ops:
  6.5 32.8 %copy-start = (bf16[8,8,128,128]{3,2,1,0:T(8,128)(2,1)S(1)}, bf16[8,8,128,128]{3,2,1,0:T(8,128)(2,1)}, u32[]{:S(2)}) copy-start(bf16[8,8,128,128]{3,2,1,0:T(8,128)(2,1)} %param.22) | copy-start | bytes 6291460
  10.3 11.8 %all-to-all-start = ((s32[4,1,8]{2,1,0:T(1,128)}), s32[4,1,8]{2,1,0:T(1,128)S(1)}, u32[]{:S(2)}, u32[]{:S(2)}) async-start(s32[4,1,8]{2,1,0:T(1,128)} %bitcast.1), calls=%async_computation | async-start | bytes 4096 | tf_op jit(solution)/shard_map/all_to_all | solution.py:56
  22.1 16.8 %all-to-all-start.1 = ((bf16[4,8,8192]{2,1,0:T(8,128)(2,1)}), bf16[4,8,8192]{2,1,0:T(8,128)(2,1)S(1)}, u32[]{:S(2)}, u32[]{:S(2)}) async-start(bf16[4,8,8192]{2,1,0:T(8,128)(2,1)} %fusion), calls=%async_computation.1 | async-start | bytes 1048576 | tf_op jit(solution)/shard_map/all_to_all | solution.py:55
  25.6 8.2 %copy-start.3 = (s32[8,8]{1,0:T(8,128)S(1)}, s32[8,8]{1,0:T(8,128)}, u32[]{:S(2)}) copy-start(s32[8,8]{1,0:T(8,128)} %param.23) | copy-start | bytes 772
  33.7 11.4 %copy-start.2 = (bf16[2,2,1024]{2,1,0:T(2,128)(2,1)S(1)}, bf16[2,2,1024]{2,1,0:T(2,128)(2,1)}, u32[]{:S(2)}) copy-start(bf16[2,2,1024]{2,1,0:T(2,128)(2,1)} %param.18) | copy-start | bytes 24580
  33.7 21.9 %copy-start.5 = (s32[2]{0:T(128)S(1)}, s32[2]{0:T(128)}, u32[]{:S(2)}) copy-start(s32[2]{0:T(128)} %param.19) | copy-start | bytes 28
  41.8 9.2 %all-to-all-start.2 = ((f32[4,8,1024]{2,1,0:T(8,128)}), f32[4,8,1024]{2,1,0:T(8,128)S(1)}, u32[]{:S(2)}, u32[]{:S(2)}) async-start(f32[4,8,1024]{2,1,0:T(8,128)} %reshape_reshape.13), calls=%async_computation.2 | async-start | bytes 262144 | tf_op jit(solution)/shard_map/all_to_all | solution.py:71
  51.8 8.6 %all-to-all-start.3 = ((bf16[8,2,1024]{2,1,0:T(2,128)(2,1)}), bf16[8,2,1024]{2,1,0:T(2,128)(2,1)S(1)}, u32[]{:S(2)}, u32[]{:S(2)}) async-start(bf16[8,2,1024]{2,1,0:T(2,128)(2,1)} %all_to_all.49), calls=%async_computation.3 | async-start | bytes 65536 | tf_op jit(solution)/shard_map/all_to_all | solution.py:137
  60.4 4.0 %copy-start.1 = (bf16[2,8,1024,128]{3,2,1,0:T(8,128)(2,1)S(1)}, bf16[2,8,1024,128]{3,2,1,0:T(8,128)(2,1)}, u32[]{:S(2)}) copy-start(bf16[2,8,1024,128]{3,2,1,0:T(8,128)(2,1)} %param.17) | copy-start | bytes 12582916
  60.6 8.7 %copy-start.4 = (s32[8,8]{1,0:T(8,128)S(1)}, s32[8,8]{1,0:T(8,128)}, u32[]{:S(2)}) copy-start(s32[8,8]{1,0:T(8,128)} %param.25) | copy-start | bytes 772
  65.9 8.1 %all-to-all-start.4 = ((bf16[2,8,1024]{2,0,1:T(2,128)(2,1)}), bf16[2,8,1024]{2,0,1:T(2,128)(2,1)S(1)}, u32[]{:S(2)}, u32[]{:S(2)}) async-start(bf16[2,8,1024]{2,0,1:T(2,128)(2,1)} %copy.28), calls=%async_computation.4 | async-start | bytes 65536 | tf_op jit(solution)/shard_map/all_to_all | solution.py:139
  74.9 9.0 %all-to-all-start.5 = ((bf16[4,8,1024]{2,1,0:T(8,128)(2,1)}), bf16[4,8,1024]{2,1,0:T(8,128)(2,1)S(1)}, u32[]{:S(2)}, u32[]{:S(2)}) async-start(bf16[4,8,1024]{2,1,0:T(8,128)(2,1)} %fusion.6), calls=%async_computation.5 | async-start | bytes 131072 | tf_op jit(solution)/shard_map/all_to_all | solution.py:55
  89.1 28.2 %all-to-all-start.6 = ((f32[4,8,8192]{2,1,0:T(8,128)}), f32[4,8,8192]{2,1,0:T(8,128)S(1)}, u32[]{:S(2)}, u32[]{:S(2)}) async-start(f32[4,8,8192]{2,1,0:T(8,128)} %reshape_reshape.15), calls=%async_computation.6 | async-start | bytes 2097152 | tf_op jit(solution)/shard_map/all_to_all | solution.py:71
  92.6 58.9 %reduce-scatter.2.cloned.1.call-start = ((), (), s32[]{:S(2)}) async-start(), calls=%async_computation.8 | async-start | bytes 589824 | tf_op jit(solution)/shard_map/reduce_scatter | solution.py:145
Sparse Core Ops, SparseCore 0:
  119.8 31.6 reduce-scatter.1
where the time goes:
time: 161 us; the launch traced here: 160 us
  waiting for transfers between devices  75.4 us (47%)
  matrix products  33.2 us (21%)
  starting transfers between devices  27.2 us (17%)
  between operations  13.6 us (8%)
  local copies, waits for them, and re-layouts  6.09 us (4%)
  other arithmetic  4.35 us (3%)
    reduce_scatter x1, waiting for transfers between devices, body(): lax.psum_scatter(partial_terms, 'tensor', scatter_dimension=1, tiled=True)  31.8 us
    all_to_all x2, waiting for transfers between devices, return_home(): lax.all_to_all(result, 'dp', split_axis=0, concat_axis=0, tiled=True)  21.4 us
    all_to_all x2, waiting for transfers between devices, visit_store(): lax.all_to_all(packed, 'dp', split_axis=0, concat_axis=0, tiled=True)  9.39 us
    dot_general x1, matrix products, body(): jnp.dot(heads_out, output_weight, preferred_element_type=jnp.float32)  8.91 us
    dot_general x1, matrix products, body(): jnp.dot(activations, query_weight, preferred_element_type=jnp.float32)  8.14 us
    all_to_all x2, starting transfers between devices, return_home(): lax.all_to_all(result, 'dp', split_axis=0, concat_axis=0, tiled=True)  6.84 us
    all_to_all x2, starting transfers between devices, visit_store(): lax.all_to_all(packed, 'dp', split_axis=0, concat_axis=0, tiled=True)  6.75 us
    all_to_all x1, starting transfers between devices, visit_store(): lax.all_to_all(slot_sent, 'dp', split_axis=0, concat_axis=0, tiled=True)  6.32 us
  transfers between devices with their start and end apart: 8, of which 8 were waited for; matrix products, arithmetic and copies ran while one was open for 13% of the time, Pallas kernels for 0%

commit v1 on v0

v1 whole, which is shorter than its diff:
```python
import functools

import jax
import jax.numpy as jnp
from jax import lax
from jax.experimental import pallas as pl
from jax.experimental.pallas import tpu as pltpu
from jax.sharding import PartitionSpec as P

LANES = 128
CAP = 8
F32 = jnp.float32
BF16 = jnp.bfloat16


def kernel(
    dims,
    act_ref,
    fresh_ref,
    length_ref,
    tenant_ref,
    table_ref,
    qwhere_ref,
    owhere_ref,
    qw_hbm,
    ow_hbm,
    key_hbm,
    value_hbm,
    qd_hbm,
    od_hbm,
    out_ref,
    qw,
    ow,
    keys,
    values,
    qd,
    od,
    info,
    acc,
    pack_out,
    pack_in,
    back_out,
    back_in,
    head_rows,
    q_out,
    q_in,
    extra_out,
    extra_in,
    a_out,
    a_in,
    part,
    sum_out,
    sum_in,
    qw_sem,
    ow_sem,
    cache_sem,
    delta_sem,
    dp_send,
    dp_recv,
    tp_send,
    tp_recv,
    all_send,
    all_recv,
):
    stores, shards, group, rows, width, tiles, slots, context = dims
    heads = width // LANES
    all_tiles = act_ref.shape[1] // LANES
    half = tiles // 2
    dp = lax.axis_index("dp")
    tp = lax.axis_index("tensor")
    chunk = qw.shape[0] // shards
    message = a_out.dtype
    compact = stores * CAP

    def peer_of(axis, step):
        me, count = (dp, stores) if axis == "dp" else (tp, shards)
        return lax.rem(me + step, count)

    qd_copy = pltpu.make_async_copy(qd_hbm, qd, delta_sem.at[0])
    od_copy = pltpu.make_async_copy(od_hbm, od, delta_sem.at[1])
    key_copy = pltpu.make_async_copy(key_hbm, keys, cache_sem.at[0])
    value_copy = pltpu.make_async_copy(value_hbm, values, cache_sem.at[1])

    def qw_copy(c):
        span = pl.ds(pl.multiple_of(c * chunk, chunk), chunk)
        return pltpu.make_async_copy(qw_hbm.at[span], qw.at[span], qw_sem.at[c])

    def ow_copy(c):
        span = pl.ds(pl.multiple_of(c * width, width), width)
        return pltpu.make_async_copy(ow_hbm.at[:, span], ow.at[c], ow_sem.at[c])

    def start_all(copy):
        def step(c, carry):
            copy(c).start()
            return carry

        lax.fori_loop(0, shards, step, 0)

    barrier = pltpu.get_barrier_semaphore()
    for far in range(stores):
        for step in range(shards):
            if far or step:
                pl.semaphore_signal(
                    barrier,
                    inc=1,
                    device_id={"dp": peer_of("dp", far), "tensor": peer_of("tensor", step)},
                    device_id_type=pl.DeviceIdType.MESH,
                )
    start_all(qw_copy)
    qd_copy.start()

    lane = lax.broadcasted_iota(jnp.int32, (group, LANES), 1)
    row = lax.broadcasted_iota(jnp.int32, (group, LANES), 0)
    slot = jnp.zeros((group, LANES), jnp.int32)
    for r in range(group):
        slot = jnp.where(row == r, table_ref[tenant_ref[r]], slot)
    info[dp] = jnp.zeros(info.shape[1:], jnp.int32)
    info[dp, 0:slots, 0:tiles] = qwhere_ref[...]
    info[dp, 0:slots, tiles : 2 * tiles] = owhere_ref[...]
    info[dp, slots : slots + group, :] = slot
    acc[...] = jnp.zeros_like(acc)
    pl.semaphore_wait(barrier, stores * shards - 1)

    def send(axis, phase, step, src, dst):
        sems = (dp_send, dp_recv) if axis == "dp" else (tp_send, tp_recv)
        copy = pltpu.make_async_remote_copy(
            src_ref=src,
            dst_ref=dst,
            send_sem=sems[0].at[phase, step],
            recv_sem=sems[1].at[phase, step],
            device_id={axis: peer_of(axis, step)},
            device_id_type=pl.DeviceIdType.MESH,
        )
        copy.start()
        return copy

    sent = []

    def exchange(axis, phase, src, dst):
        me, count = (dp, stores) if axis == "dp" else (tp, shards)
        copies = [
            send(axis, phase, step, src(peer_of(axis, step)), dst.at[me])
            for step in range(1, count)
        ]
        sent.extend(copies)
        return copies

    def scatter(phase, src, dst, steps, over):
        copies = []
        for step in steps:
            peer = peer_of("tensor", step)
            for far in reversed(range(over)):
                if step == 0 and far == 0:
                    continue
                to = peer_of("dp", far)
                copy = pltpu.make_async_remote_copy(
                    src_ref=src(to, peer),
                    dst_ref=dst.at[dp, tp],
                    send_sem=all_send.at[phase, far, step],
                    recv_sem=all_recv.at[phase, far, step],
                    device_id={"dp": to, "tensor": peer},
                    device_id_type=pl.DeviceIdType.MESH,
                )
                copy.start()
                copies.append(copy)
        sent.extend(copies)
        return copies

    def arrive(copies):
        for copy in copies:
            copy.wait_recv()

    info_copies = exchange("dp", 0, lambda peer: info.at[dp], info)

    def base_query(first, last):
        def step(c, carry):
            qw_copy(c).wait()
            span = pl.ds(pl.multiple_of(c * chunk, chunk), chunk)
            acc[...] += jnp.dot(act_ref[:, span], qw[span, :], preferred_element_type=F32)
            return carry

        lax.fori_loop(first, last, step, 0)

    store = jnp.zeros((group, LANES), jnp.int32)
    for index in range(1, stores):
        store = store + jnp.where(slot >= index * slots, 1, 0)
    of_store = lane == store
    row_i = lax.broadcasted_iota(jnp.int32, (group, group), 0)
    row_j = lax.broadcasted_iota(jnp.int32, (group, group), 1)
    earlier = jnp.where(row_j < row_i, 1.0, 0.0).astype(F32)
    rank = jnp.dot(earlier, jnp.where(of_store, 1.0, 0.0).astype(F32), preferred_element_type=F32)
    rank = jnp.sum(jnp.where(of_store, rank, 0.0), axis=1, keepdims=True)
    place = store.astype(F32) * CAP + rank
    home = jnp.where(lane.astype(F32) == place, 1.0, 0.0).astype(F32)
    home = home[:, : stores * CAP]
    outward = home.T.astype(BF16)
    homeward = home.astype(BF16)

    def pack(picked, out):
        packed = jnp.dot(outward, jnp.concatenate(picked, axis=1), preferred_element_type=F32)
        packed = packed.reshape(stores, CAP, tiles * LANES)
        low = packed[:, :, : half * LANES]
        high = packed[:, :, half * LANES :]
        out[...] = jnp.concatenate([low, high], axis=1).astype(BF16)

    def products(taken, deltas):
        results = []
        for k in range(tiles):
            x = jnp.concatenate([jnp.where(m, taken[k], 0.0) for m in own_slot], axis=1)
            w = deltas[:, k].reshape(slots * LANES, LANES)
            results.append(jnp.dot(x.astype(BF16), w, preferred_element_type=F32))
        return results

    def returned(back):
        got = back[...].astype(F32)
        low = got[:, :CAP].reshape(stores * CAP, half * LANES)
        high = got[:, CAP:].reshape(stores * CAP, half * LANES)
        rows_in = jnp.concatenate([low, high], axis=1).astype(BF16)
        return jnp.dot(homeward, rows_in, preferred_element_type=F32)

    def spread(terms, targets, column):
        total = jnp.where(targets[0] == column, terms[0], 0.0)
        for k in range(1, tiles):
            total += jnp.where(targets[k] == column, terms[k], 0.0)
        return total

    def lanes_of(table, k):
        return jnp.broadcast_to(table[:, k : k + 1], table.shape)

    base_query(0, shards // 4)
    key_copy.start()
    value_copy.start()

    arrive(info_copies)
    where = jnp.zeros((group, LANES), jnp.int32)
    for d in range(stores):
        for s in range(slots):
            where = where + jnp.where(slot == d * slots + s, info[d, s : s + 1, :], 0)
    q_place = [lanes_of(where, k) for k in range(tiles)]
    o_place = [lanes_of(where, tiles + k) for k in range(tiles)]
    head_shift = heads.bit_length() - 1
    tile_shift = all_tiles.bit_length() - 1
    q_source = [lax.shift_right_logical(p, head_shift) for p in q_place]
    o_target = [p & (all_tiles - 1) for p in o_place]

    picked = [jnp.zeros((group, LANES), F32) for _ in range(tiles)]
    for t in range(all_tiles):
        block = act_ref[:, t * LANES : (t + 1) * LANES].astype(F32)
        picked = [jnp.where(q_source[k] == t, block, picked[k]) for k in range(tiles)]
    pack([p.astype(BF16) for p in picked], pack_out)
    pack_in[dp] = pack_out[dp]
    pack_copies = exchange("dp", 1, lambda peer: pack_out.at[peer], pack_in)

    picks = []
    marks = []
    for g in range(stores):
        theirs = info[g, slots : slots + group, :]
        mine = (theirs >= dp * slots) & (theirs < (dp + 1) * slots)
        before = jnp.dot(earlier, jnp.where(mine, 1.0, 0.0), preferred_element_type=F32)
        pick = mine & (lane.astype(F32) == before + g * CAP)
        picks.append(jnp.where(pick, 1.0, 0.0))
        marks.append((theirs - dp * slots + 1).astype(F32))
    expand = jnp.concatenate(picks, axis=0)[:, :compact]
    gather = expand.T
    mark = jnp.dot(gather, jnp.concatenate(marks, axis=0), preferred_element_type=F32)
    expand = expand.astype(BF16)
    gather = gather.astype(BF16)
    own_slot = [mark == s + 1 for s in range(slots)]
    near = jnp.zeros((compact, LANES), jnp.int32)
    for s in range(slots):
        near = near + jnp.where(own_slot[s], info[dp, s : s + 1, :], 0)
    near_target = [lanes_of(near, k) & (heads - 1) for k in range(tiles)]
    near_source = [
        lax.shift_right_logical(lanes_of(near, tiles + k), tile_shift) for k in range(tiles)
    ]

    base_query(shards // 4, shards)
    od_copy.start()
    start_all(ow_copy)
    for h in range(heads):
        head_rows[dp, :, h, :] = acc[:, h * LANES : (h + 1) * LANES]
    q_out[...] = head_rows[dp].reshape(shards, rows * heads, LANES)
    q_in[tp] = q_out[tp]
    q_copies = exchange("tensor", 0, lambda peer: q_out.at[peer], q_in)

    qd_copy.wait()
    arrive(pack_copies)
    got = pack_in[...].astype(F32)
    taken = []
    for k in range(tiles):
        start = CAP * (k // half)
        column = (k % half) * LANES
        x = got[:, start : start + CAP, column : column + LANES]
        taken.append(x.reshape(compact, LANES))
    terms = products(taken, qd)
    placed = jnp.concatenate([spread(terms, near_target, h) for h in range(heads)], axis=1)
    placed = jnp.dot(expand, placed.astype(BF16), preferred_element_type=F32)
    placed = placed.reshape(stores, group, width)
    for h in range(heads):
        head_rows[:, :, h, :] = placed[:, :, h * LANES : (h + 1) * LANES]
    extra = head_rows[...].reshape(stores, shards, rows * heads, LANES)
    extra_out[...] = extra.astype(BF16).astype(message)
    extra_in[dp, tp] = extra_out[dp, tp]
    extra_copies = scatter(
        0, lambda to, peer: extra_out.at[to, peer], extra_in, range(shards), stores
    )

    scale = LANES ** (-0.5)
    lines = rows * heads
    line = lax.broadcasted_iota(jnp.int32, (lines, 1), 0)
    of_row = [(line >= r * heads) & (line < (r + 1) * heads) for r in range(rows)]
    limit = jnp.zeros((lines, 1), jnp.int32)
    for r in range(rows):
        limit = jnp.where(of_row[r], length_ref[r], limit)
    visible = lax.broadcasted_iota(jnp.int32, (lines, context), 1) < limit
    kv_heads = keys.shape[1]

    key_copy.wait()
    value_copy.wait()
    arrive(q_copies)
    arrive(extra_copies)

    def attend(step):
        j = peer_of("tensor", step)
        g = j * kv_heads // shards
        q32 = q_in[j]
        for d in range(stores):
            q32 = q32 + extra_in[d, j].astype(F32)
        q = q32.astype(BF16)
        q32 = q.astype(F32)
        fresh_key = jnp.zeros((lines, LANES), F32)
        fresh_value = jnp.zeros((lines, LANES), F32)
        scores = None
        for r in range(rows):
            here = pl.ds(pl.multiple_of(g * LANES, LANES), LANES)
            fresh = fresh_ref[r, :, here].astype(F32)
            fresh_key = jnp.where(of_row[r], fresh[0:1], fresh_key)
            fresh_value = jnp.where(of_row[r], fresh[1:2], fresh_value)
            one = lax.dot_general(
                q, keys[r, g], (((1,), (1,)), ((), ())), preferred_element_type=F32
            )
            scores = one if scores is None else jnp.where(of_row[r], one, scores)
        own = jnp.sum(q32 * fresh_key, axis=1, keepdims=True) * scale
        scores = jnp.where(visible, scores * scale, -1e30)
        highest = jnp.maximum(jnp.max(scores, axis=1, keepdims=True), own)
        weights = jnp.where(visible, jnp.exp(scores - highest), 0.0)
        own_weight = jnp.exp(own - highest)
        inverse = 1.0 / (jnp.sum(weights, axis=1, keepdims=True) + own_weight)
        chance = (weights * inverse).astype(BF16)
        own_chance = (own_weight * inverse).astype(BF16).astype(F32)
        mixed = None
        for r in range(rows):
            one = jnp.dot(chance, values[r, g], preferred_element_type=F32)
            mixed = one if mixed is None else jnp.where(of_row[r], one, mixed)
        mixed = mixed + own_chance * fresh_value
        a_out[j] = mixed.astype(BF16).astype(message)

    a_copies = []
    parts = [range(0, shards // 2), range(shards // 2, shards)]
    for steps in parts:
        for step in steps:
            attend(step)
        a_copies += scatter(1, lambda to, peer: a_out.at[peer], a_in, steps, stores)
    a_in[dp, tp] = a_out[tp]
    arrive(a_copies)
    head_rows[...] = a_in[...].astype(F32).reshape(stores, group, heads, LANES)
    blocks = [head_rows[:, :, h, :].reshape(stores * group, LANES) for h in range(heads)]
    blocks = jnp.concatenate([b.astype(BF16) for b in blocks], axis=1)
    blocks = jnp.dot(gather, blocks, preferred_element_type=F32)
    taken = []
    for k in range(tiles):
        one = jnp.zeros((compact, LANES), F32)
        for h in range(heads):
            one = jnp.where(near_source[k] == h, blocks[:, h * LANES : (h + 1) * LANES], one)
        taken.append(one)
    od_copy.wait()
    terms = products(taken, od)
    low = jnp.concatenate(terms[:half], axis=1).reshape(stores, CAP, half * LANES)
    high = jnp.concatenate(terms[half:], axis=1).reshape(stores, CAP, half * LANES)
    back_out[...] = jnp.concatenate([low, high], axis=1).astype(BF16)
    back_in[dp] = back_out[dp]
    back_copies = exchange("dp", 2, lambda peer: back_out.at[peer], back_in)
    attended = jnp.concatenate([head_rows[dp, :, h, :].astype(BF16) for h in range(heads)], axis=1)

    def base_out(first, last):
        def step(c, carry):
            ow_copy(c).wait()
            part[c] = jnp.dot(attended, ow[c], preferred_element_type=F32)
            return carry

        lax.fori_loop(first, last, step, 0)

    base_out(0, shards)
    arrive(back_copies)
    terms = returned(back_in)
    terms = [terms[:, k * LANES : (k + 1) * LANES] for k in range(tiles)]

    def whole_part(owner):
        extra = [spread(terms, o_target, owner * heads + h) for h in range(heads)]
        return part[owner] + jnp.concatenate(extra, axis=1)

    sum_copies = []
    for step in range(1, shards):
        owner = peer_of("tensor", step)
        sum_out[step] = whole_part(owner).astype(BF16)
        sum_copies.append(send("tensor", 1, step, sum_out.at[step], sum_in.at[step]))
    sent.extend(sum_copies)
    total = whole_part(tp)
    for step in range(1, shards):
        sum_copies[step - 1].wait_recv()
        total = total + sum_in[step].astype(F32)
    out_ref[...] = total.astype(BF16)
    for copy in sent:
        copy.wait_send()


def body(
    activations,
    query_weight,
    output_weight,
    key_cache,
    value_cache,
    fresh_pair,
    cache_length,
    row_tenant,
    tenant_slot,
    query_deltas,
    query_where,
    output_deltas,
    output_where,
):
    stores = lax.axis_size("dp")
    shards = lax.axis_size("tensor")
    group = activations.shape[0]
    rows = key_cache.shape[0]
    width = query_weight.shape[1]
    slots, tiles = query_where.shape
    context = key_cache.shape[2]
    heads = width // LANES
    lines = rows * heads
    message = BF16 if lines % 16 == 0 else F32
    dims = (stores, shards, group, rows, width, tiles, slots, context)
    pack_shape = (stores, 2 * CAP, tiles // 2 * LANES)
    all_shape = (stores, shards, lines, LANES)
    vmem = pl.BlockSpec(memory_space=pltpu.VMEM)
    smem = pl.BlockSpec(memory_space=pltpu.SMEM)
    anywhere = pl.BlockSpec(memory_space=pl.ANY)
    return pl.pallas_call(
        functools.partial(kernel, dims),
        out_shape=jax.ShapeDtypeStruct((group, width), BF16),
        in_specs=[vmem, vmem, smem, smem, smem, vmem, vmem] + [anywhere] * 6,
        out_specs=vmem,
        scratch_shapes=[
            pltpu.VMEM(query_weight.shape, BF16),
            pltpu.VMEM((shards, width, width), BF16),
            pltpu.VMEM(key_cache.shape, BF16),
            pltpu.VMEM(value_cache.shape, BF16),
            pltpu.VMEM(query_deltas.shape, BF16),
            pltpu.VMEM(output_deltas.shape, BF16),
            pltpu.VMEM((stores, slots + group, LANES), jnp.int32),
            pltpu.VMEM((group, width), F32),
            pltpu.VMEM(pack_shape, BF16),
            pltpu.VMEM(pack_shape, BF16),
            pltpu.VMEM(pack_shape, BF16),
            pltpu.VMEM(pack_shape, BF16),
            pltpu.VMEM((stores, group, heads, LANES), F32),
            pltpu.VMEM((shards, lines, LANES), F32),
            pltpu.VMEM((shards, lines, LANES), F32),
            pltpu.VMEM(all_shape, message),
            pltpu.VMEM(all_shape, message),
            pltpu.VMEM((shards, lines, LANES), message),
            pltpu.VMEM(all_shape, message),
            pltpu.VMEM((shards, group, width), F32),
            pltpu.VMEM((shards, group, width), BF16),
            pltpu.VMEM((shards, group, width), BF16),
            pltpu.SemaphoreType.DMA((shards,)),
            pltpu.SemaphoreType.DMA((shards,)),
            pltpu.SemaphoreType.DMA((2,)),
            pltpu.SemaphoreType.DMA((2,)),
            pltpu.SemaphoreType.DMA((3, stores)),
            pltpu.SemaphoreType.DMA((3, stores)),
            pltpu.SemaphoreType.DMA((2, shards)),
            pltpu.SemaphoreType.DMA((2, shards)),
            pltpu.SemaphoreType.DMA((2, stores, shards)),
            pltpu.SemaphoreType.DMA((2, stores, shards)),
        ],
        compiler_params=pltpu.CompilerParams(
            collective_id=0, has_side_effects=True, vmem_limit_bytes=56 * 1024 * 1024
        ),
        name="decode_layer",
    )(
        activations,
        fresh_pair,
        cache_length,
        row_tenant,
        tenant_slot,
        query_where,
        output_where,
        query_weight,
        output_weight,
        key_cache,
        value_cache,
        query_deltas,
        output_deltas,
    )


def solution(mesh):
    placed = (
        P("dp", None),
        P(None, "tensor"),
        P("tensor", None),
        P(("dp", "tensor"), None, None, None),
        P(("dp", "tensor"), None, None, None),
        P(("dp", "tensor"), None, None),
        P(("dp", "tensor")),
        P("dp"),
        P(),
        P("dp", "tensor", None, None),
        P("dp", "tensor"),
        P("dp", "tensor", None, None),
        P("dp", "tensor"),
    )
    return jax.shard_map(
        body, mesh=mesh, in_specs=placed, out_specs=P("dp", "tensor"), check_vma=False
    )
```

time: 161 us -> 43.1 us (0.27)
  waiting for transfers between devices: 75.4 us -> 0 us
  Pallas kernels: 0 us -> 41.5 us
  matrix products: 33.2 us -> 0 us
  starting transfers between devices: 27.2 us -> 0 us
  between operations: 13.6 us -> 0.01 us
  local copies, waits for them, and re-layouts: 6.09 us -> 1.38 us
  other arithmetic: 4.35 us -> 0 us
    all_to_all x7 -> x0, waiting for transfers between devices: 43.6 us -> none  [the longest x2 21.4 us: return_home(): lax.all_to_all(result, 'dp', split_axis=0, concat_axis=0, tiled=True)]
    pallas_call x0 -> x1, Pallas kernels: none -> 41.5 us  [body(): pl.pallas_call(functools.partial(kernel, dims), out_shape=jax.ShapeDtypeS...]
    dot_general x15 -> x0, matrix products: 33.2 us -> none  [the longest x1 8.91 us: body(): jnp.dot(heads_out, output_weight, preferred_element_type=jnp.float32)]
    reduce_scatter x1 -> x0, waiting for transfers between devices: 31.8 us -> none  [body(): lax.psum_scatter(partial_terms, 'tensor', scatter_dimension=1, tiled=True)]
    all_to_all x7 -> x0, starting transfers between devices: 27 us -> none  [the longest x2 6.84 us: return_home(): lax.all_to_all(result, 'dp', split_axis=0, concat_axis=0, tiled=True)]
    all_to_all x6 -> x0, local copies, waits for them, and re-layouts: 2.51 us -> none  [the longest x2 1.18 us: visit_store(): lax.all_to_all(slot_sent, 'dp', split_axis=0, concat_axis=0, tiled=True)]
    another operation x2 -> x0, local copies, waits for them, and re-layouts: 1.84 us -> none  [visit_store(): return result.reshape(stores, capacity, out_columns)]
  transfers between devices with their start and end apart: 8 -> 0, of which waited for: 8 -> 0; matrix products, arithmetic and copies ran while one was open for 13% -> 0% of each run, Pallas kernels for 0% -> 0%
where the time goes in v1:
time: 43.1 us; the launch traced here: 42.9 us
  Pallas kernels  41.5 us (96%)
  local copies, waits for them, and re-layouts  1.38 us (3%)
    pallas_call x1, Pallas kernels, body(): pl.pallas_call(functools.partial(kernel, dims), out_shape=jax.ShapeDtypeS...  41.5 us
    unnamed x1, local copies, waits for them, and re-layouts  1.38 us

profile of v1, /device:TPU:0, one launch (start us, length us, event | category | flops | bytes accessed | tf_op | source)
XLA Modules:
  0.0 42.9 jit_solution(8449164458860526197)
XLA Ops:
  0.0 41.5 %decode_layer.1 = bf16[16,1024]{1,0:T(8,128)(2,1)} custom-call(bf16[16,8192]{1,0:T(8,128)(2,1)} %act_ref.1, bf16[2,2,1024]{2,1,0:T(2,128)(2,1)} %fresh_ref.1, s32[2]{0:T(128)} %length_ref.1, s32[16]{0:T(128)} %tenant_ref.1, s32[32]{0:T(128)} %table_ref.1, s32[8,8]{1,0:T(8,128)} %qwhere_ref.1, s32[8,8]{1,0:T(8,128)} %owhere_ref.1, bf16[8192,1024]{1,0:T(8,128)(2,1)} %qw_hbm.1, ...), custom_call_target="tpu_custom_call" | custom-call | tf_op jit(solution)/shard_map/decode_layer/pallas_call | solution.py:448
  41.5 1.4 %copy.15 = bf16[16,1024]{1,0:T(8,128)(2,1)} copy(bf16[16,1024]{1,0:T(8,128)(2,1)} %decode_layer.1) | data formatting | bytes 65536

commit v2 on v1

--- a/solution.py
+++ b/solution.py
@@ -72,9 +72,13 @@
     message = a_out.dtype
     compact = stores * CAP
 
+    peers = {
+        "dp": [dp] + [lax.rem(dp + step, stores) for step in range(1, stores)],
+        "tensor": [tp] + [lax.rem(tp + step, shards) for step in range(1, shards)],
+    }
+
     def peer_of(axis, step):
-        me, count = (dp, stores) if axis == "dp" else (tp, shards)
-        return lax.rem(me + step, count)
+        return peers[axis][step]
 
     qd_copy = pltpu.make_async_copy(qd_hbm, qd, delta_sem.at[0])
     od_copy = pltpu.make_async_copy(od_hbm, od, delta_sem.at[1])
@@ -97,15 +101,11 @@
         lax.fori_loop(0, shards, step, 0)
 
     barrier = pltpu.get_barrier_semaphore()
-    for far in range(stores):
-        for step in range(shards):
-            if far or step:
-                pl.semaphore_signal(
-                    barrier,
-                    inc=1,
-                    device_id={"dp": peer_of("dp", far), "tensor": peer_of("tensor", step)},
-                    device_id_type=pl.DeviceIdType.MESH,
-                )
+    for axis in ("dp", "tensor"):
+        for peer in peers[axis][1:]:
+            pl.semaphore_signal(
+                barrier, inc=1, device_id={axis: peer}, device_id_type=pl.DeviceIdType.MESH
+            )
     start_all(qw_copy)
     qd_copy.start()
 
@@ -119,7 +119,7 @@
     info[dp, 0:slots, tiles : 2 * tiles] = owhere_ref[...]
     info[dp, slots : slots + group, :] = slot
     acc[...] = jnp.zeros_like(acc)
-    pl.semaphore_wait(barrier, stores * shards - 1)
+    pl.semaphore_wait(barrier, stores - 1 + shards - 1)
 
     def send(axis, phase, step, src, dst):
         sems = (dp_send, dp_recv) if axis == "dp" else (tp_send, tp_recv)
@@ -145,11 +145,11 @@
         sent.extend(copies)
         return copies
 
-    def scatter(phase, src, dst, steps, over):
-        copies = []
+    def scatter(phase, src, dst, steps):
+        copies = {}
         for step in steps:
             peer = peer_of("tensor", step)
-            for far in reversed(range(over)):
+            for far in reversed(range(stores)):
                 if step == 0 and far == 0:
                     continue
                 to = peer_of("dp", far)
@@ -162,8 +162,8 @@
                     device_id_type=pl.DeviceIdType.MESH,
                 )
                 copy.start()
-                copies.append(copy)
-        sent.extend(copies)
+                copies[far, step] = copy
+        sent.extend(copies.values())
         return copies
 
     def arrive(copies):
@@ -301,8 +301,9 @@
     extra = head_rows[...].reshape(stores, shards, rows * heads, LANES)
     extra_out[...] = extra.astype(BF16).astype(message)
     extra_in[dp, tp] = extra_out[dp, tp]
+    order = [0] + list(range(shards - 1, 0, -1))
     extra_copies = scatter(
-        0, lambda to, peer: extra_out.at[to, peer], extra_in, range(shards), stores
+        0, lambda to, peer: extra_out.at[to, peer], extra_in, range(shards)
     )
 
     scale = LANES ** (-0.5)
@@ -318,7 +319,6 @@
     key_copy.wait()
     value_copy.wait()
     arrive(q_copies)
-    arrive(extra_copies)
 
     def attend(step):
         j = peer_of("tensor", step)
@@ -355,14 +355,29 @@
         mixed = mixed + own_chance * fresh_value
         a_out[j] = mixed.astype(BF16).astype(message)
 
-    a_copies = []
-    parts = [range(0, shards // 2), range(shards // 2, shards)]
-    for steps in parts:
+    a_copies = {}
+    for steps in (order[: shards // 2], order[shards // 2 :]):
+        for step in steps:
+            source = (shards - step) % shards
+            arrive([extra_copies[far, source] for far in range(stores) if far or source])
         for step in steps:
             attend(step)
-        a_copies += scatter(1, lambda to, peer: a_out.at[peer], a_in, steps, stores)
+        a_copies.update(scatter(1, lambda to, peer: a_out.at[peer], a_in, steps))
     a_in[dp, tp] = a_out[tp]
-    arrive(a_copies)
+
+    def base_out(first, last):
+        def step(c, carry):
+            ow_copy(c).wait()
+            part[c] = jnp.dot(attended, ow[c], preferred_element_type=F32)
+            return carry
+
+        lax.fori_loop(first, last, step, 0)
+
+    arrive([copy for (far, step), copy in a_copies.items() if far == 0])
+    head_rows[dp] = a_in[dp].astype(F32).reshape(group, heads, LANES)
+    attended = jnp.concatenate([head_rows[dp, :, h, :].astype(BF16) for h in range(heads)], axis=1)
+    base_out(0, shards // 2)
+    arrive([copy for (far, step), copy in a_copies.items() if far > 0])
     head_rows[...] = a_in[...].astype(F32).reshape(stores, group, heads, LANES)
     blocks = [head_rows[:, :, h, :].reshape(stores * group, LANES) for h in range(heads)]
     blocks = jnp.concatenate([b.astype(BF16) for b in blocks], axis=1)
@@ -380,17 +395,9 @@
     back_out[...] = jnp.concatenate([low, high], axis=1).astype(BF16)
     back_in[dp] = back_out[dp]
     back_copies = exchange("dp", 2, lambda peer: back_out.at[peer], back_in)
-    attended = jnp.concatenate([head_rows[dp, :, h, :].astype(BF16) for h in range(heads)], axis=1)
-
-    def base_out(first, last):
-        def step(c, carry):
-            ow_copy(c).wait()
-            part[c] = jnp.dot(attended, ow[c], preferred_element_type=F32)
-            return carry
-
-        lax.fori_loop(first, last, step, 0)
-
-    base_out(0, shards)
+    base_out(shards // 2, shards)
+    for copy in sent:
+        copy.wait_send()
     arrive(back_copies)
     terms = returned(back_in)
     terms = [terms[:, k * LANES : (k + 1) * LANES] for k in range(tiles)]
@@ -404,13 +411,12 @@
         owner = peer_of("tensor", step)
         sum_out[step] = whole_part(owner).astype(BF16)
         sum_copies.append(send("tensor", 1, step, sum_out.at[step], sum_in.at[step]))
-    sent.extend(sum_copies)
     total = whole_part(tp)
     for step in range(1, shards):
         sum_copies[step - 1].wait_recv()
         total = total + sum_in[step].astype(F32)
     out_ref[...] = total.astype(BF16)
-    for copy in sent:
+    for copy in sum_copies:
         copy.wait_send()
 
 

time: 43.1 us -> 41.4 us (0.961)
  Pallas kernels: 41.5 us -> 39.8 us
    pallas_call x1, Pallas kernels: 41.5 us -> 39.8 us  [body(): pl.pallas_call(functools.partial(kernel, dims), out_shape=jax.ShapeDtypeS...]
where the time goes in v2:
time: 41.4 us; the launch traced here: 41.2 us
  Pallas kernels  39.8 us (96%)
  local copies, waits for them, and re-layouts  1.38 us (3%)
    pallas_call x1, Pallas kernels, body(): pl.pallas_call(functools.partial(kernel, dims), out_shape=jax.ShapeDtypeS...  39.8 us
    unnamed x1, local copies, waits for them, and re-layouts  1.38 us

profile of v2, /device:TPU:0, one launch (start us, length us, event | category | flops | bytes accessed | tf_op | source)
XLA Modules:
  0.0 41.2 jit_solution(14175166084098390857)
XLA Ops:
  0.0 39.8 %decode_layer.1 = bf16[16,1024]{1,0:T(8,128)(2,1)} custom-call(bf16[16,8192]{1,0:T(8,128)(2,1)} %act_ref.1, bf16[2,2,1024]{2,1,0:T(2,128)(2,1)} %fresh_ref.1, s32[2]{0:T(128)} %length_ref.1, s32[16]{0:T(128)} %tenant_ref.1, s32[32]{0:T(128)} %table_ref.1, s32[8,8]{1,0:T(8,128)} %qwhere_ref.1, s32[8,8]{1,0:T(8,128)} %owhere_ref.1, bf16[8192,1024]{1,0:T(8,128)(2,1)} %qw_hbm.1, ...), custom_call_target="tpu_custom_call" | custom-call | tf_op jit(solution)/shard_map/decode_layer/pallas_call | solution.py:454
  39.8 1.4 %copy.15 = bf16[16,1024]{1,0:T(8,128)(2,1)} copy(bf16[16,1024]{1,0:T(8,128)(2,1)} %decode_layer.1) | data formatting | bytes 65536

commit v3 on v2

--- a/solution.py
+++ b/solution.py
@@ -61,6 +61,10 @@
     tp_recv,
     all_send,
     all_recv,
+    pair_out,
+    pair_in,
+    pair_send,
+    pair_recv,
 ):
     stores, shards, group, rows, width, tiles, slots, context = dims
     heads = width // LANES
@@ -71,6 +75,9 @@
     chunk = qw.shape[0] // shards
     message = a_out.dtype
     compact = stores * CAP
+    half_width = width // 2
+    parity = lax.rem(dp, 2)
+    partner = dp + 1 - 2 * parity
 
     peers = {
         "dp": [dp] + [lax.rem(dp + step, stores) for step in range(1, stores)],
@@ -90,7 +97,9 @@
         return pltpu.make_async_copy(qw_hbm.at[span], qw.at[span], qw_sem.at[c])
 
     def ow_copy(c):
-        span = pl.ds(pl.multiple_of(c * width, width), width)
+        owner = lax.rem(tp + c, shards)
+        start = owner * width + parity * half_width
+        span = pl.ds(pl.multiple_of(start, half_width), half_width)
         return pltpu.make_async_copy(ow_hbm.at[:, span], ow.at[c], ow_sem.at[c])
 
     def start_all(copy):
@@ -274,14 +283,9 @@
         lax.shift_right_logical(lanes_of(near, tiles + k), tile_shift) for k in range(tiles)
     ]
 
-    base_query(shards // 4, shards)
+    base_query(shards // 4, 3 * shards // 4)
     od_copy.start()
     start_all(ow_copy)
-    for h in range(heads):
-        head_rows[dp, :, h, :] = acc[:, h * LANES : (h + 1) * LANES]
-    q_out[...] = head_rows[dp].reshape(shards, rows * heads, LANES)
-    q_in[tp] = q_out[tp]
-    q_copies = exchange("tensor", 0, lambda peer: q_out.at[peer], q_in)
 
     qd_copy.wait()
     arrive(pack_copies)
@@ -305,6 +309,13 @@
     extra_copies = scatter(
         0, lambda to, peer: extra_out.at[to, peer], extra_in, range(shards)
     )
+
+    base_query(3 * shards // 4, shards)
+    for h in range(heads):
+        head_rows[dp, :, h, :] = acc[:, h * LANES : (h + 1) * LANES]
+    q_out[...] = head_rows[dp].reshape(shards, rows * heads, LANES)
+    q_in[tp] = q_out[tp]
+    q_copies = exchange("tensor", 0, lambda peer: q_out.at[peer], q_in)
 
     scale = LANES ** (-0.5)
     lines = rows * heads
@@ -365,19 +376,28 @@
         a_copies.update(scatter(1, lambda to, peer: a_out.at[peer], a_in, steps))
     a_in[dp, tp] = a_out[tp]
 
-    def base_out(first, last):
+    def pair_copy(c):
+        return pltpu.make_async_remote_copy(
+            src_ref=pair_out.at[c],
+            dst_ref=pair_in.at[c],
+            send_sem=pair_send.at[c],
+            recv_sem=pair_recv.at[c],
+            device_id={"dp": partner, "tensor": lax.rem(tp + c, shards)},
+            device_id_type=pl.DeviceIdType.MESH,
+        )
+
+    def base_out():
         def step(c, carry):
             ow_copy(c).wait()
-            part[c] = jnp.dot(attended, ow[c], preferred_element_type=F32)
+            both = jnp.dot(attended, ow[c], preferred_element_type=F32)
+            part[c] = both.reshape(2, group, half_width)
+            pair_out[c] = part[c, 1 - parity].astype(BF16)
+            pair_copy(c).start()
             return carry
 
-        lax.fori_loop(first, last, step, 0)
-
-    arrive([copy for (far, step), copy in a_copies.items() if far == 0])
-    head_rows[dp] = a_in[dp].astype(F32).reshape(group, heads, LANES)
-    attended = jnp.concatenate([head_rows[dp, :, h, :].astype(BF16) for h in range(heads)], axis=1)
-    base_out(0, shards // 2)
-    arrive([copy for (far, step), copy in a_copies.items() if far > 0])
+        lax.fori_loop(0, shards, step, 0)
+
+    arrive(list(a_copies.values()))
     head_rows[...] = a_in[...].astype(F32).reshape(stores, group, heads, LANES)
     blocks = [head_rows[:, :, h, :].reshape(stores * group, LANES) for h in range(heads)]
     blocks = jnp.concatenate([b.astype(BF16) for b in blocks], axis=1)
@@ -395,29 +415,45 @@
     back_out[...] = jnp.concatenate([low, high], axis=1).astype(BF16)
     back_in[dp] = back_out[dp]
     back_copies = exchange("dp", 2, lambda peer: back_out.at[peer], back_in)
-    base_out(shards // 2, shards)
+    pair = pl.ds(dp - parity, 2)
+    attended = [head_rows[pair, :, h, :].reshape(2 * group, LANES) for h in range(heads)]
+    attended = jnp.concatenate([a.astype(BF16) for a in attended], axis=1)
+    base_out()
     for copy in sent:
         copy.wait_send()
     arrive(back_copies)
     terms = returned(back_in)
     terms = [terms[:, k * LANES : (k + 1) * LANES] for k in range(tiles)]
 
-    def whole_part(owner):
+    low_half = (1 - parity).astype(F32)
+    high_half = parity.astype(F32)
+
+    def whole_part(step):
+        owner = peer_of("tensor", step)
         extra = [spread(terms, o_target, owner * heads + h) for h in range(heads)]
-        return part[owner] + jnp.concatenate(extra, axis=1)
+        base = part[step, parity]
+        return jnp.concatenate(extra, axis=1) + jnp.concatenate(
+            [base * low_half, base * high_half], axis=1
+        )
 
     sum_copies = []
     for step in range(1, shards):
-        owner = peer_of("tensor", step)
-        sum_out[step] = whole_part(owner).astype(BF16)
+        sum_out[step] = whole_part(step).astype(BF16)
         sum_copies.append(send("tensor", 1, step, sum_out.at[step], sum_in.at[step]))
-    total = whole_part(tp)
+    total = whole_part(0)
+    others = jnp.zeros((group, half_width), F32)
+    for c in range(shards):
+        pair_copy(c).wait_recv()
+        others = others + pair_in[c].astype(F32)
+    total = total + jnp.concatenate([others * high_half, others * low_half], axis=1)
     for step in range(1, shards):
         sum_copies[step - 1].wait_recv()
         total = total + sum_in[step].astype(F32)
     out_ref[...] = total.astype(BF16)
     for copy in sum_copies:
         copy.wait_send()
+    for c in range(shards):
+        pair_copy(c).wait_send()
 
 
 def body(
@@ -458,7 +494,7 @@
         out_specs=vmem,
         scratch_shapes=[
             pltpu.VMEM(query_weight.shape, BF16),
-            pltpu.VMEM((shards, width, width), BF16),
+            pltpu.VMEM((shards, width, width // 2), BF16),
             pltpu.VMEM(key_cache.shape, BF16),
             pltpu.VMEM(value_cache.shape, BF16),
             pltpu.VMEM(query_deltas.shape, BF16),
@@ -476,7 +512,7 @@
             pltpu.VMEM(all_shape, message),
             pltpu.VMEM((shards, lines, LANES), message),
             pltpu.VMEM(all_shape, message),
-            pltpu.VMEM((shards, group, width), F32),
+            pltpu.VMEM((shards, 2, group, width // 2), F32),
             pltpu.VMEM((shards, group, width), BF16),
             pltpu.VMEM((shards, group, width), BF16),
             pltpu.SemaphoreType.DMA((shards,)),
@@ -489,6 +525,10 @@
             pltpu.SemaphoreType.DMA((2, shards)),
             pltpu.SemaphoreType.DMA((2, stores, shards)),
             pltpu.SemaphoreType.DMA((2, stores, shards)),
+            pltpu.VMEM((shards, group, width // 2), BF16),
+            pltpu.VMEM((shards, group, width // 2), BF16),
+            pltpu.SemaphoreType.DMA((shards,)),
+            pltpu.SemaphoreType.DMA((shards,)),
         ],
         compiler_params=pltpu.CompilerParams(
             collective_id=0, has_side_effects=True, vmem_limit_bytes=56 * 1024 * 1024

time: 41.4 us -> 41.6 us (level)
  no operation moved by 1% of the time
where the time goes in v3:
time: 41.6 us; the launch traced here: 41.4 us
  Pallas kernels  40 us (96%)
  local copies, waits for them, and re-layouts  1.38 us (3%)
    pallas_call x1, Pallas kernels, body(): pl.pallas_call(functools.partial(kernel, dims), out_shape=jax.ShapeDtypeS...  40 us
    unnamed x1, local copies, waits for them, and re-layouts  1.38 us

profile of v3, /device:TPU:0, one launch (start us, length us, event | category | flops | bytes accessed | tf_op | source)
XLA Modules:
  0.0 41.4 jit_solution(7937879096294042024)
XLA Ops:
  0.0 40.0 %decode_layer.1 = bf16[16,1024]{1,0:T(8,128)(2,1)} custom-call(bf16[16,8192]{1,0:T(8,128)(2,1)} %act_ref.1, bf16[2,2,1024]{2,1,0:T(2,128)(2,1)} %fresh_ref.1, s32[2]{0:T(128)} %length_ref.1, s32[16]{0:T(128)} %tenant_ref.1, s32[32]{0:T(128)} %table_ref.1, s32[8,8]{1,0:T(8,128)} %qwhere_ref.1, s32[8,8]{1,0:T(8,128)} %owhere_ref.1, bf16[8192,1024]{1,0:T(8,128)(2,1)} %qw_hbm.1, ...), custom_call_target="tpu_custom_call" | custom-call | tf_op jit(solution)/shard_map/decode_layer/pallas_call | solution.py:490
  40.1 1.4 %copy.15 = bf16[16,1024]{1,0:T(8,128)(2,1)} copy(bf16[16,1024]{1,0:T(8,128)(2,1)} %decode_layer.1) | data formatting | bytes 65536

commit v4 on v3

--- a/solution.py
+++ b/solution.py
@@ -214,10 +214,14 @@
 
     def products(taken, deltas):
         results = []
-        for k in range(tiles):
-            x = jnp.concatenate([jnp.where(m, taken[k], 0.0) for m in own_slot], axis=1)
-            w = deltas[:, k].reshape(slots * LANES, LANES)
-            results.append(jnp.dot(x.astype(BF16), w, preferred_element_type=F32))
+        for k in range(0, tiles, 2):
+            x = jnp.concatenate(taken[k : k + 2], axis=0)
+            x = jnp.concatenate([jnp.where(m, x, 0.0) for m in own_slot], axis=1)
+            w = [deltas[:, k + i].reshape(slots * LANES, LANES) for i in range(2)]
+            both = jnp.dot(
+                x.astype(BF16), jnp.concatenate(w, axis=1), preferred_element_type=F32
+            )
+            results += [both[:compact, :LANES], both[compact:, LANES:]]
         return results
 
     def returned(back):
@@ -276,14 +280,16 @@
     gather = gather.astype(BF16)
     own_slot = [mark == s + 1 for s in range(slots)]
     near = jnp.zeros((compact, LANES), jnp.int32)
+    one_slot = own_slot
+    own_slot = [jnp.concatenate([mark, mark], axis=0) == s + 1 for s in range(slots)]
     for s in range(slots):
-        near = near + jnp.where(own_slot[s], info[dp, s : s + 1, :], 0)
+        near = near + jnp.where(one_slot[s], info[dp, s : s + 1, :], 0)
     near_target = [lanes_of(near, k) & (heads - 1) for k in range(tiles)]
     near_source = [
         lax.shift_right_logical(lanes_of(near, tiles + k), tile_shift) for k in range(tiles)
     ]
 
-    base_query(shards // 4, 3 * shards // 4)
+    base_query(shards // 4, 7 * shards // 8)
     od_copy.start()
     start_all(ow_copy)
 
@@ -310,7 +316,7 @@
         0, lambda to, peer: extra_out.at[to, peer], extra_in, range(shards)
     )
 
-    base_query(3 * shards // 4, shards)
+    base_query(7 * shards // 8, shards)
     for h in range(heads):
         head_rows[dp, :, h, :] = acc[:, h * LANES : (h + 1) * LANES]
     q_out[...] = head_rows[dp].reshape(shards, rows * heads, LANES)
@@ -337,20 +343,21 @@
         q32 = q_in[j]
         for d in range(stores):
             q32 = q32 + extra_in[d, j].astype(F32)
-        q = q32.astype(BF16)
-        q32 = q.astype(F32)
+        q32 = q32.astype(BF16).astype(F32)
         fresh_key = jnp.zeros((lines, LANES), F32)
         fresh_value = jnp.zeros((lines, LANES), F32)
-        scores = None
         for r in range(rows):
             here = pl.ds(pl.multiple_of(g * LANES, LANES), LANES)
             fresh = fresh_ref[r, :, here].astype(F32)
             fresh_key = jnp.where(of_row[r], fresh[0:1], fresh_key)
             fresh_value = jnp.where(of_row[r], fresh[1:2], fresh_value)
-            one = lax.dot_general(
-                q, keys[r, g], (((1,), (1,)), ((), ())), preferred_element_type=F32
-            )
-            scores = one if scores is None else jnp.where(of_row[r], one, scores)
+        apart = [jnp.where(of_row[r], q32, 0.0).astype(BF16) for r in range(rows)]
+        scores = lax.dot_general(
+            jnp.concatenate(apart, axis=1),
+            jnp.concatenate([keys[r, g] for r in range(rows)], axis=1),
+            (((1,), (1,)), ((), ())),
+            preferred_element_type=F32,
+        )
         own = jnp.sum(q32 * fresh_key, axis=1, keepdims=True) * scale
         scores = jnp.where(visible, scores * scale, -1e30)
         highest = jnp.maximum(jnp.max(scores, axis=1, keepdims=True), own)
@@ -359,10 +366,11 @@
         inverse = 1.0 / (jnp.sum(weights, axis=1, keepdims=True) + own_weight)
         chance = (weights * inverse).astype(BF16)
         own_chance = (own_weight * inverse).astype(BF16).astype(F32)
-        mixed = None
-        for r in range(rows):
-            one = jnp.dot(chance, values[r, g], preferred_element_type=F32)
-            mixed = one if mixed is None else jnp.where(of_row[r], one, mixed)
+        side = jnp.concatenate([values[r, g] for r in range(rows)], axis=1)
+        side = jnp.dot(chance, side, preferred_element_type=F32)
+        mixed = side[:, :LANES]
+        for r in range(1, rows):
+            mixed = jnp.where(of_row[r], side[:, r * LANES : (r + 1) * LANES], mixed)
         mixed = mixed + own_chance * fresh_value
         a_out[j] = mixed.astype(BF16).astype(message)
 
@@ -386,7 +394,7 @@
             device_id_type=pl.DeviceIdType.MESH,
         )
 
-    def base_out():
+    def base_out(first, last):
         def step(c, carry):
             ow_copy(c).wait()
             both = jnp.dot(attended, ow[c], preferred_element_type=F32)
@@ -395,9 +403,30 @@
             pair_copy(c).start()
             return carry
 
-        lax.fori_loop(0, shards, step, 0)
-
-    arrive(list(a_copies.values()))
+        lax.fori_loop(first, last, step, 0)
+
+    def arrive_from(far):
+        for step in range(shards):
+            pltpu.make_async_remote_copy(
+                src_ref=a_out.at[0],
+                dst_ref=a_in.at[dp, tp],
+                send_sem=all_send.at[1, far, step],
+                recv_sem=all_recv.at[1, far, step],
+                device_id={"dp": partner, "tensor": tp},
+                device_id_type=pl.DeviceIdType.MESH,
+            ).wait_recv()
+
+    near_far = parity + (1 - parity) * (stores - 1)
+    arrive([copy for (far, step), copy in a_copies.items() if far == 0])
+    arrive_from(near_far)
+    pair = pl.ds(dp - parity, 2)
+    head_rows[pair] = a_in[pair].astype(F32).reshape(2, group, heads, LANES)
+    attended = [head_rows[pair, :, h, :].reshape(2 * group, LANES) for h in range(heads)]
+    attended = jnp.concatenate([a.astype(BF16) for a in attended], axis=1)
+    base_out(0, shards // 4)
+    arrive_from(stores - near_far)
+    for far in range(2, stores - 1):
+        arrive_from(far)
     head_rows[...] = a_in[...].astype(F32).reshape(stores, group, heads, LANES)
     blocks = [head_rows[:, :, h, :].reshape(stores * group, LANES) for h in range(heads)]
     blocks = jnp.concatenate([b.astype(BF16) for b in blocks], axis=1)
@@ -415,10 +444,7 @@
     back_out[...] = jnp.concatenate([low, high], axis=1).astype(BF16)
     back_in[dp] = back_out[dp]
     back_copies = exchange("dp", 2, lambda peer: back_out.at[peer], back_in)
-    pair = pl.ds(dp - parity, 2)
-    attended = [head_rows[pair, :, h, :].reshape(2 * group, LANES) for h in range(heads)]
-    attended = jnp.concatenate([a.astype(BF16) for a in attended], axis=1)
-    base_out()
+    base_out(shards // 4, shards)
     for copy in sent:
         copy.wait_send()
     arrive(back_copies)

time: 41.6 us -> 41.6 us (level)
  no operation moved by 1% of the time
where the time goes in v4:
time: 41.6 us; the launch traced here: 41.4 us
  Pallas kernels  40 us (96%)
  local copies, waits for them, and re-layouts  1.38 us (3%)
    pallas_call x1, Pallas kernels, body(): pl.pallas_call(functools.partial(kernel, dims), out_shape=jax.ShapeDtypeS...  40 us
    unnamed x1, local copies, waits for them, and re-layouts  1.38 us

profile of v4, /device:TPU:0, one launch (start us, length us, event | category | flops | bytes accessed | tf_op | source)
XLA Modules:
  0.0 41.4 jit_solution(46031898150270706)
XLA Ops:
  0.0 40.0 %decode_layer.1 = bf16[16,1024]{1,0:T(8,128)(2,1)} custom-call(bf16[16,8192]{1,0:T(8,128)(2,1)} %act_ref.1, bf16[2,2,1024]{2,1,0:T(2,128)(2,1)} %fresh_ref.1, s32[2]{0:T(128)} %length_ref.1, s32[16]{0:T(128)} %tenant_ref.1, s32[32]{0:T(128)} %table_ref.1, s32[8,8]{1,0:T(8,128)} %qwhere_ref.1, s32[8,8]{1,0:T(8,128)} %owhere_ref.1, bf16[8192,1024]{1,0:T(8,128)(2,1)} %qw_hbm.1, ...), custom_call_target="tpu_custom_call" | custom-call | tf_op jit(solution)/shard_map/decode_layer/pallas_call | solution.py:516
  40.0 1.4 %copy.15 = bf16[16,1024]{1,0:T(8,128)(2,1)} copy(bf16[16,1024]{1,0:T(8,128)(2,1)} %decode_layer.1) | data formatting | bytes 65536

commit v5 on v3

--- a/solution.py
+++ b/solution.py
@@ -283,9 +283,15 @@
         lax.shift_right_logical(lanes_of(near, tiles + k), tile_shift) for k in range(tiles)
     ]
 
-    base_query(shards // 4, 3 * shards // 4)
+    base_query(shards // 4, shards)
     od_copy.start()
     start_all(ow_copy)
+    for h in range(heads):
+        head_rows[dp, :, h, :] = acc[:, h * LANES : (h + 1) * LANES]
+    q_out[...] = head_rows[dp].reshape(shards, rows * heads, LANES)
+    q_in[tp] = q_out[tp]
+    q_copies = exchange("tensor", 0, lambda peer: q_out.at[peer], q_in)
+
 
     qd_copy.wait()
     arrive(pack_copies)
@@ -309,13 +315,6 @@
     extra_copies = scatter(
         0, lambda to, peer: extra_out.at[to, peer], extra_in, range(shards)
     )
-
-    base_query(3 * shards // 4, shards)
-    for h in range(heads):
-        head_rows[dp, :, h, :] = acc[:, h * LANES : (h + 1) * LANES]
-    q_out[...] = head_rows[dp].reshape(shards, rows * heads, LANES)
-    q_in[tp] = q_out[tp]
-    q_copies = exchange("tensor", 0, lambda peer: q_out.at[peer], q_in)
 
     scale = LANES ** (-0.5)
     lines = rows * heads
@@ -386,7 +385,7 @@
             device_id_type=pl.DeviceIdType.MESH,
         )
 
-    def base_out():
+    def base_out(first, last):
         def step(c, carry):
             ow_copy(c).wait()
             both = jnp.dot(attended, ow[c], preferred_element_type=F32)
@@ -395,9 +394,30 @@
             pair_copy(c).start()
             return carry
 
-        lax.fori_loop(0, shards, step, 0)
-
-    arrive(list(a_copies.values()))
+        lax.fori_loop(first, last, step, 0)
+
+    def arrive_from(far):
+        for step in range(shards):
+            pltpu.make_async_remote_copy(
+                src_ref=a_out.at[0],
+                dst_ref=a_in.at[dp, tp],
+                send_sem=all_send.at[1, far, step],
+                recv_sem=all_recv.at[1, far, step],
+                device_id={"dp": partner, "tensor": tp},
+                device_id_type=pl.DeviceIdType.MESH,
+            ).wait_recv()
+
+    near_far = parity + (1 - parity) * (stores - 1)
+    arrive([copy for (far, step), copy in a_copies.items() if far == 0])
+    arrive_from(near_far)
+    pair = pl.ds(dp - parity, 2)
+    head_rows[pair] = a_in[pair].astype(F32).reshape(2, group, heads, LANES)
+    attended = [head_rows[pair, :, h, :].reshape(2 * group, LANES) for h in range(heads)]
+    attended = jnp.concatenate([a.astype(BF16) for a in attended], axis=1)
+    base_out(0, shards // 4)
+    arrive_from(stores - near_far)
+    for far in range(2, stores - 1):
+        arrive_from(far)
     head_rows[...] = a_in[...].astype(F32).reshape(stores, group, heads, LANES)
     blocks = [head_rows[:, :, h, :].reshape(stores * group, LANES) for h in range(heads)]
     blocks = jnp.concatenate([b.astype(BF16) for b in blocks], axis=1)
@@ -415,10 +435,7 @@
     back_out[...] = jnp.concatenate([low, high], axis=1).astype(BF16)
     back_in[dp] = back_out[dp]
     back_copies = exchange("dp", 2, lambda peer: back_out.at[peer], back_in)
-    pair = pl.ds(dp - parity, 2)
-    attended = [head_rows[pair, :, h, :].reshape(2 * group, LANES) for h in range(heads)]
-    attended = jnp.concatenate([a.astype(BF16) for a in attended], axis=1)
-    base_out()
+    base_out(shards // 4, shards)
     for copy in sent:
         copy.wait_send()
     arrive(back_copies)

time: 41.6 us -> 41.6 us (level)
  no operation moved by 1% of the time
where the time goes in v5:
time: 41.6 us; the launch traced here: 41.4 us
  Pallas kernels  40 us (96%)
  local copies, waits for them, and re-layouts  1.38 us (3%)
    pallas_call x1, Pallas kernels, body(): pl.pallas_call(functools.partial(kernel, dims), out_shape=jax.ShapeDtypeS...  40 us
    unnamed x1, local copies, waits for them, and re-layouts  1.38 us

profile of v5, /device:TPU:0, one launch (start us, length us, event | category | flops | bytes accessed | tf_op | source)
XLA Modules:
  0.0 41.4 jit_solution(11661059320584044957)
XLA Ops:
  0.0 40.0 %decode_layer.1 = bf16[16,1024]{1,0:T(8,128)(2,1)} custom-call(bf16[16,8192]{1,0:T(8,128)(2,1)} %act_ref.1, bf16[2,2,1024]{2,1,0:T(2,128)(2,1)} %fresh_ref.1, s32[2]{0:T(128)} %length_ref.1, s32[16]{0:T(128)} %tenant_ref.1, s32[32]{0:T(128)} %table_ref.1, s32[8,8]{1,0:T(8,128)} %qwhere_ref.1, s32[8,8]{1,0:T(8,128)} %owhere_ref.1, bf16[8192,1024]{1,0:T(8,128)(2,1)} %qw_hbm.1, ...), custom_call_target="tpu_custom_call" | custom-call | tf_op jit(solution)/shard_map/decode_layer/pallas_call | solution.py:507
  40.0 1.4 %copy.15 = bf16[16,1024]{1,0:T(8,128)(2,1)} copy(bf16[16,1024]{1,0:T(8,128)(2,1)} %decode_layer.1) | data formatting | bytes 65536
